TPU v7x, 32 devices: a whole 2x2x4 slice. The times are simulated.
32 devices in a mesh: mol: 2 (over y), amp: 4 (over z), summa: 2 (over x), rep: 2 (over core).
Axes of the slice: x: 2, y: 2, z: 4, core: 2. Of those that a mesh axis runs over, the one named last changes fastest.
Arguments:
- integrals: float32 [200, 512, 4, 100], P(('mol', 'summa'), ('amp', 'rep')), parts along dimension 0, may hold values from -0.078125 to 0.078125
- amplitudes: float32 [200, 64, 512, 100], P(('mol', 'summa'), ('amp', 'rep')), parts along dimension 0, may hold values from -6 to 6
- occ_irreps: int32 [200], P('mol'), parts along dimension 0, may hold values from 0 to 7
- virt_irreps: int32 [16], P('mol'), parts along dimension 0, may hold values from 0 to 7
Outputs:
- cycle: float32 [8, 100, 64, 100], P(('mol', 'summa'), None, ('amp', 'rep')), parts along dimension 0
There are 2 independent parts, one for each index of `mol`. A program takes and returns all parts, laid end to end along the dimension named above; each array names one. Nothing has to cross between parts.
All inputs are finite; a program needn't handle non-finite values.
Results may differ from a plain program's by a relative error of at most 0.00007.
Values sent between devices are 32-bit elements; how exact they have to be, the bound alone decides.
No kernel may reach another device: no remote copies, remote signals or barrier semaphores. Data moves between devices by JAX's collectives and lax.ppermute only.
A program may use at most 384 MiB of HBM per device.

v0:
```python
import jax
import jax.numpy as jnp
from jax import lax
from jax.sharding import PartitionSpec as P

TILE = 64


def contract(weights, amp_rows):
    return jnp.einsum(
        "kcai,kbcj->aibj",
        weights,
        amp_rows,
        precision=lax.Precision.HIGHEST,
        preferred_element_type=jnp.float32,
    )


def body(integrals, amplitudes, occ_irreps, virt_irreps):
    k_local = integrals.shape[0]
    k_first = lax.axis_index("summa") * k_local
    panel = lax.all_gather(integrals, ("amp", "rep"), axis=1, tiled=True)
    c_count = panel.shape[1]
    occ_labels = lax.dynamic_slice_in_dim(occ_irreps, k_first, k_local)
    tile_ids = jnp.arange(c_count, dtype=jnp.int32) // TILE
    onehot = tile_ids[:, None] == jnp.arange(virt_irreps.shape[0], dtype=jnp.int32)[None, :]
    virt_labels = jnp.sum(jnp.where(onehot, virt_irreps[None, :], 0), axis=1)
    masked = (
        panel * (occ_labels[:, None] == virt_labels[None, :]).astype(jnp.float32)[:, :, None, None]
    )
    partial_value = contract(masked, amplitudes)
    return lax.psum_scatter(partial_value, "summa", scatter_dimension=0, tiled=True)


def solution(mesh):
    return jax.shard_map(
        body,
        mesh=mesh,
        in_specs=(
            P(("mol", "summa"), ("amp", "rep"), None, None),
            P(("mol", "summa"), ("amp", "rep"), None, None),
            P("mol"),
            P("mol"),
        ),
        out_specs=P(("mol", "summa"), None, ("amp", "rep"), None),
        check_vma=False,
    )
```

profile of v0, /device:TPU:26, one launch (start us, length us, event | category | flops | bytes accessed | tf_op | source)
XLA Modules:
  0.0 877.5 jit_solution(6413689742594990078)
XLA Ops:
  6.5 0.0 all-gather.2.cloned.1.call-start
  6.5 0.7 all-gather.2.cloned.1.call-update
  7.3 0.0 reduce-scatter.2.cloned.1.call-start
  7.3 0.7 dynamic_slice.3
  8.0 0.7 select_reduce_fusion
  8.8 0.1 compare_convert_fusion
  8.9 442.7 %all-gather.2.cloned.1.call-done = f32[50,512,4,100]{3,2,1,0:T(4,128)} async-done(((f32[50,64,4,100]{3,2,1,0:T(4,128)}), f32[50,512,4,100]{3,2,1,0:T(4,128)}) %all-gather.2.cloned.1.call-update) | async-done | bytes 40960016 | tf_op jit(solution)/shard_map/all_gather | solution.py:22
  451.6 34.5 %multiply_bitcast_fusion = f32[50,512,4,100,1]{3,2,1,0,4:T(4,128)} fusion(f32[50,512,4,100]{3,2,1,0:T(4,128)} %all-gather.2.cloned.1.call-done, f32[50,512]{1,0:T(8,128)S(1)} %compare_convert_fusion), kind=kLoop, calls=%fused_computation.4 | loop fusion | flops 10240000 | bytes 82022400 | tf_op jit(solution)/shard_map/mul | solution.py:29
  486.1 354.6 %fusion.4 = f32[4,100,8,100]{3,1,2,0:T(8,128)} fusion(f32[50,8,512,100]{2,1,3,0:T(8,128)} %param.5, f32[50,512,4,100,1]{3,2,1,0,4:T(4,128)} %multiply_bitcast_fusion), kind=kOutput, calls=%fused_computation.5 | convolution fusion | flops 98304000000 | bytes 124160000 | tf_op jit(solution)/shard_map/kcai,kbcj->aibj/dot_general | solution.py:10
  840.7 0.0 reduce-scatter.2.cloned.1.call-update
  840.7 27.8 %reduce-scatter.2.cloned.1.call-done = f32[2,100,8,100]{3,1,2,0:T(8,128)} async-done(((f32[4,100,8,100]{3,1,2,0:T(8,128)}), f32[2,100,8,100]{3,1,2,0:T(8,128)}) %reduce-scatter.2.cloned.1.call-update) | async-done | bytes 640016 | tf_op jit(solution)/shard_map/reduce_scatter | solution.py:32
  868.5 2.2 copy.10
  (1 shorter events, 0.0 us)
Async XLA Ops:
  6.5 445.0 %all-gather.2.cloned.1.call-start = ((), (), s32[]{:S(2)}) async-start(), calls=%async_computation.1 | async-start | bytes 58982400 | tf_op jit(solution)/shard_map/all_gather | solution.py:22
  7.3 861.2 %reduce-scatter.2.cloned.1.call-start = ((), (), s32[]{:S(2)}) async-start(), calls=%async_computation.2 | async-start | bytes 2555904 | tf_op jit(solution)/shard_map/reduce_scatter | solution.py:32
Sparse Core Ops, SparseCore 0:
  9.0 442.5 all-gather.1
  840.8 27.6 reduce-scatter.1
where the time goes:
time: 880 us; the launch traced here: 878 us
  waiting for transfers between devices  471 us (54%)
  matrix products  355 us (40%)
  other arithmetic  35.3 us (4%)
  between operations  13.4 us (2%)
    all_gather x1, waiting for transfers between devices, body(): panel = lax.all_gather(integrals, ('amp', 'rep'), axis=1, tiled=True)  443 us
    dot_general x1, matrix products, contract(): jnp.einsum('kcai,kbcj->aibj', weights, amp_rows, precision=lax.Precision....  355 us
    mul x1, other arithmetic, body(): panel * (occ_labels[:, None] == virt_labels[None, :]).astype(jnp.float32)...  34.5 us
    reduce_scatter x1, waiting for transfers between devices, body(): lax.psum_scatter(partial_value, 'summa', scatter_dimension=0, tiled=True)  27.8 us
  transfers between devices with their start and end apart: 2, of which 2 were waited for; matrix products, arithmetic and copies ran while one was open for 0% of the time, Pallas kernels for 0%

commit v1 on v0

v1 whole, which is shorter than its diff:
```python
import functools

import jax
import jax.numpy as jnp
from jax import lax
from jax.experimental import pallas as pl
from jax.experimental.pallas import tpu as pltpu
from jax.sharding import PartitionSpec as P

CAP = 12
DEPTH = 4
LANES = 128
VMEM_LIMIT = 40 * 1024 * 1024


def round_up(value, unit):
    return -(-value // unit) * unit


def pack_kernel(groups, ent_ref, me_ref, src_ref, out_ref, buf, sems):
    slots, c_blk, rows_a, inner = buf.shape
    blocks = src_ref.shape[1] // c_blk
    per_group = rows_a // groups
    me = me_ref[0]

    def copy(slot):
        ent = ent_ref[slot]
        return pltpu.make_async_copy(
            src_ref.at[ent // blocks, pl.ds(pl.multiple_of((ent % blocks) * c_blk, c_blk), c_blk)],
            buf.at[slot],
            sems.at[slot],
        )

    @pl.loop(0, slots)
    def _(slot):
        @pl.when(ent_ref[slot] >= 0)
        def _():
            copy(slot).start()

    @pl.loop(0, slots)
    def _(slot):
        @pl.when(ent_ref[slot] >= 0)
        def _():
            copy(slot).wait()
            for a in range(rows_a):
                phase = lax.rem(a // per_group - me + groups, groups)
                lane = (a % per_group) * c_blk
                out_ref[phase, slot, :inner, lane : lane + c_blk] = buf[slot, :, a, :].T


def pack(integrals, ent, me, groups, c_blk):
    _, _, rows_a, inner = integrals.shape
    slots = ent.shape[0]
    smem = pl.BlockSpec(memory_space=pltpu.SMEM)
    return pl.pallas_call(
        functools.partial(pack_kernel, groups),
        out_shape=jax.ShapeDtypeStruct(
            (groups, slots, round_up(inner, 8), rows_a // groups * c_blk), jnp.float32
        ),
        in_specs=[smem, smem, pl.BlockSpec(memory_space=pl.ANY)],
        out_specs=pl.BlockSpec(memory_space=pltpu.VMEM),
        scratch_shapes=[
            pltpu.VMEM((slots, c_blk, rows_a, inner), jnp.float32),
            pltpu.SemaphoreType.DMA((slots,)),
        ],
        compiler_params=pltpu.CompilerParams(vmem_limit_bytes=VMEM_LIMIT),
        name="pack_pairs",
    )(ent, me, integrals)


def contract_kernel(views, final, c_blk, n_acc, ent_ref, off_ref, *refs):
    n_src = len(views)
    srcs, amp_ref, adds, out_ref = refs[:n_src], refs[n_src], refs[n_src + 1 : n_src + 1 + n_acc], refs[n_src + 1 + n_acc]
    wall, tbuf, rhs, todo, wsem, tsem, *rest = refs[n_src + 2 + n_acc :]
    acc = rest[0] if final else out_ref
    slots, inner = wall.shape[:2]
    _, cols_j, cols_b, window = tbuf.shape
    per_group = acc.shape[2] // LANES

    copies = []
    base = 0
    for i, (ref, lead) in enumerate(zip(srcs, views)):
        view = ref.at[lead] if lead else ref
        count = ref.shape[len(lead)]
        copies.append(pltpu.make_async_copy(view, wall.at[pl.ds(base, count)], wsem.at[i]))
        copies[-1].start()
        base += count

    def note(slot, found):
        @pl.when(ent_ref[slot] >= 0)
        def _():
            todo[found] = slot

        return found + (ent_ref[slot] >= 0).astype(jnp.int32)

    total = lax.fori_loop(0, slots, note, jnp.int32(0))

    def fetch(i):
        slot = todo[i]
        place = lax.rem(i, DEPTH)
        first = pl.multiple_of((off_ref[slot] // window) * window, window)
        return pltpu.make_async_copy(
            amp_ref.at[ent_ref[slot], :, :, pl.ds(first, window)], tbuf.at[place], tsem.at[place]
        )

    for i in range(DEPTH - 1):

        @pl.when(i < total)
        def _():
            fetch(i).start()

    rhs[...] = jnp.zeros_like(rhs)
    if n_acc:
        value = adds[0][...]
        for one in adds[1:]:
            value += one[...]
        acc[...] = value
    else:
        acc[...] = jnp.zeros_like(acc)
    for one in copies:
        one.wait()

    @pl.loop(0, total)
    def _(i):
        @pl.when(i + DEPTH - 1 < total)
        def _():
            fetch(i + DEPTH - 1).start()

        slot = todo[i]
        w = wall[slot].T
        w_high = w.astype(jnp.bfloat16)
        w_low = (w - w_high.astype(jnp.float32)).astype(jnp.bfloat16)
        for a in range(per_group):
            cut = slice(a * c_blk, (a + 1) * c_blk)
            lane = slice(a * LANES, a * LANES + inner)
            rhs[:c_blk, lane] = w_high[cut]
            rhs[c_blk : 2 * c_blk, lane] = w_high[cut]
            rhs[2 * c_blk : 3 * c_blk, lane] = w_low[cut]
            rhs[3 * c_blk :, lane] = w_low[cut]
        fetch(i).wait()
        x = tbuf[lax.rem(i, DEPTH)].reshape(cols_j * cols_b, window)
        shift = lax.rem(off_ref[slot], window)
        lane = lax.broadcasted_iota(jnp.int32, x.shape, 1)
        if window == 2 * c_blk:
            twice = jnp.where((lane < c_blk) == (shift < c_blk), x, pltpu.roll(x, c_blk, 1))
        else:
            one = pltpu.roll(x, lax.rem(window - shift, window), 1)
            twice = jnp.where(lane < c_blk, one, pltpu.roll(one, c_blk, 1))
        high = twice.astype(jnp.bfloat16).astype(jnp.float32)
        both = jnp.where(lane < c_blk, high, twice - high).astype(jnp.bfloat16)
        both = both[:, : 2 * c_blk]
        lhs = jnp.concatenate([both, both], axis=1)
        prod = jnp.dot(lhs, rhs[...], preferred_element_type=jnp.float32)
        acc[...] += prod.reshape(acc.shape)

    if final:
        rows = out_ref.shape[1]
        for a in range(per_group):
            for b in range(cols_b):
                out_ref[a, :, b, :] = acc[:, b, a * LANES : (a + 1) * LANES].T[:rows]


def contract(sources, views, ent, off, amplitudes, c_blk, adds=(), final=None):
    _, cols_j, cols_b, _ = amplitudes.shape
    rows, lanes = sources[0].shape[-2:]
    per_group = lanes // c_blk
    slots = ent.shape[0]
    window = max(LANES, 2 * c_blk)
    held = jax.ShapeDtypeStruct((cols_j, cols_b, per_group * LANES), jnp.float32)
    smem = pl.BlockSpec(memory_space=pltpu.SMEM)
    hbm = pl.BlockSpec(memory_space=pl.ANY)
    vmem = pl.BlockSpec(memory_space=pltpu.VMEM)
    scratch = [
        pltpu.VMEM((slots, rows, lanes), jnp.float32),
        pltpu.VMEM((DEPTH, cols_j, cols_b, window), jnp.float32),
        pltpu.VMEM((4 * c_blk, per_group * LANES), jnp.bfloat16),
        pltpu.SMEM((slots,), jnp.int32),
        pltpu.SemaphoreType.DMA((len(sources),)),
        pltpu.SemaphoreType.DMA((DEPTH,)),
    ]
    if final is not None:
        scratch.append(pltpu.VMEM(held.shape, jnp.float32))
        held = jax.ShapeDtypeStruct((per_group, final, cols_b, cols_j), jnp.float32)
    return pl.pallas_call(
        functools.partial(contract_kernel, views, final is not None, c_blk, len(adds)),
        out_shape=held,
        in_specs=[smem, smem] + [hbm] * (len(sources) + 1) + [vmem] * len(adds),
        out_specs=vmem,
        scratch_shapes=scratch,
        compiler_params=pltpu.CompilerParams(vmem_limit_bytes=VMEM_LIMIT),
        cost_estimate=pl.CostEstimate(
            flops=slots * cols_j * cols_b * per_group * LANES * c_blk,
            bytes_accessed=slots * cols_j * cols_b * LANES * 2,
            transcendentals=0,
        ),
        name="contract_pairs",
    )(ent, off, *sources, amplitudes, *adds)


def body(integrals, amplitudes, occ_irreps, virt_irreps):
    k_local, c_local, rows_a, inner = integrals.shape
    groups = lax.axis_size("summa")
    parts = lax.axis_size("amp") * lax.axis_size("rep")
    me = lax.axis_index("summa")
    tile = parts * c_local // virt_irreps.shape[0]
    c_blk = min(tile, c_local)
    blocks = c_local // c_blk
    turned = jnp.transpose(amplitudes, (0, 3, 1, 2))

    occ = lax.dynamic_slice_in_dim(occ_irreps, me * k_local, k_local)
    block_labels = jnp.repeat(virt_irreps, tile // c_blk).reshape(parts, blocks)
    allowed = (occ[:, None, None] == block_labels.T[None]).reshape(k_local * blocks, parts)
    ranks = jnp.cumsum(allowed.astype(jnp.int32), axis=0)
    mine = lax.axis_index("amp") * lax.axis_size("rep") + lax.axis_index("rep")
    entry = jnp.arange(k_local * blocks, dtype=jnp.int32)

    def gather_round(start):
        wanted = start + 1 + jnp.arange(CAP, dtype=jnp.int32)
        hit = allowed[:, :, None] & (ranks[:, :, None] == wanted)
        ent = jnp.sum(jnp.where(hit, entry[:, None, None] + 1, 0), axis=0) - 1
        own = lax.dynamic_index_in_dim(ent, mine, keepdims=False)
        packed = pack(integrals, own, me[None], groups, c_blk)
        panel = lax.all_gather(packed, ("amp", "rep"))
        k_of = jnp.where(ent < 0, -1, ent // blocks).reshape(-1)
        off = jnp.arange(parts, dtype=jnp.int32)[:, None] * c_local + (ent % blocks) * c_blk
        off = jnp.where(ent < 0, 0, off).reshape(-1)
        received = []
        for phase in range(1, groups):
            views = [(d, phase) for d in range(parts)]
            value = contract([panel] * parts, views, k_of, off, turned, c_blk)
            received.append(lax.ppermute(value, "summa", [(i, (i + phase) % groups) for i in range(groups)]))
        views = [(d, 0) for d in range(parts)]
        return contract([panel] * parts, views, k_of, off, turned, c_blk, received, inner)

    everyone = (occ_irreps[:, None, None] == block_labels.T[None]).reshape(groups, -1, parts)
    most = lax.pmax(jnp.max(jnp.sum(everyone.astype(jnp.int32), axis=1)), "mol")
    first = gather_round(jnp.int32(0))

    def more(state):
        return state[0] < most

    def step(state):
        start, value = state
        return start + CAP, value + gather_round(start)

    return lax.while_loop(more, step, (jnp.int32(CAP), first))[1]


def solution(mesh):
    return jax.shard_map(
        body,
        mesh=mesh,
        in_specs=(
            P(("mol", "summa"), ("amp", "rep"), None, None),
            P(("mol", "summa"), ("amp", "rep"), None, None),
            P("mol"),
            P("mol"),
        ),
        out_specs=P(("mol", "summa"), None, ("amp", "rep"), None),
        check_vma=False,
    )
```

time: 880 us -> 211 us (0.24)
  the two profiles are of different devices: /device:TPU:26 before, /device:TPU:4 now
where the time goes in v1:
time: 211 us; the launch traced here: 209 us
  waiting for transfers between devices  113 us (54%)
  Pallas kernels  64.7 us (31%)
  between operations  13.5 us (6%)
  local copies, waits for them, and re-layouts  10.2 us (5%)
  blocking collectives  4.93 us (2%)
    all_gather x1, waiting for transfers between devices, gather_round(): panel = lax.all_gather(packed, ('amp', 'rep'))  98 us
    pallas_call x2, Pallas kernels, contract(): pl.pallas_call(functools.partial(contract_kernel, views, final is not Non...  60.3 us
    ppermute x1, waiting for transfers between devices, gather_round(): lax.ppermute(value, 'summa', [(i, (i + phase) % groups) for i in range(gr...  14.5 us
    unnamed x10, local copies, waits for them, and re-layouts  8.7 us
    pmax x1, blocking collectives, body(): most = lax.pmax(jnp.max(jnp.sum(everyone.astype(jnp.int32), axis=1)), 'mol')  4.93 us
    pallas_call x1, Pallas kernels, pack(): pl.pallas_call(functools.partial(pack_kernel, groups), out_shape=jax.Shap...  4.39 us
  transfers between devices with their start and end apart: 2, of which 2 were waited for; matrix products, arithmetic and copies ran while one was open for 1% of the time, Pallas kernels for 0%

profile of v1, /device:TPU:4, one launch (start us, length us, event | category | flops | bytes accessed | tf_op | source)
XLA Modules:
  0.0 208.5 jit_solution(18254456276943568229)
XLA Ops:
  6.5 0.0 all-gather.8.cloned.1.call-start
  6.5 0.7 dynamic_slice.15
  7.3 0.7 broadcast_compare_fusion
  8.0 0.1 copy.19
  8.1 0.1 reduce_window_sum.11
  8.2 0.1 copy.20
  8.2 0.4 select_reduce_fusion.1
  8.6 0.2 dynamic-slice_reduce_fusion.1.ent_ref
  8.8 4.4 %pack_pairs.6 = f32[2,12,104,128]{3,2,1,0:T(8,128)} custom-call(s32[12]{0:T(128)S(1)} %dynamic-slice_reduce_fusion.1.ent_ref, s32[1]{0:T(128)} %bitcast.me_ref, f32[50,64,4,100]{3,2,1,0:T(4,128)} %src_ref.1), custom_call_target="tpu_custom_call" | custom-call | tf_op jit(solution)/shard_map/pack_pairs/pallas_call | solution.py:55
  13.2 0.0 all-gather.8.cloned.1.call-update
  13.2 0.1 copy.21
  13.3 0.1 add.142
  13.4 0.1 add.143
  13.5 0.1 sub.19
  13.5 98.0 %all-gather.8.cloned.1.call-done = f32[16,12,104,128]{3,2,1,0:T(8,128)} async-done(((f32[2,12,104,128]{3,2,1,0:T(8,128)}), f32[16,12,104,128]{3,2,1,0:T(8,128)}) %all-gather.8.cloned.1.call-update) | async-done | bytes 10223632 | tf_op jit(solution)/shard_map/all_gather | solution.py:223
  111.6 0.0 copy-start.2
  111.6 3.9 %copy-done.2 = f32[16,12,104,128]{3,2,1,0:T(8,128)S(1)} copy-done((f32[16,12,104,128]{3,2,1,0:T(8,128)S(1)}, f32[16,12,104,128]{3,2,1,0:T(8,128)}, u32[]{:S(2)}) %copy-start.2) | copy-done | bytes 10223640
  115.5 0.0 copy-start.6
  115.5 0.0 copy-start.5
  115.5 29.8 %contract_pairs.12 = f32[100,8,256]{2,1,0:T(8,128)S(1)} custom-call(s32[96]{0:T(128)S(1)} %get-tuple-element.279.ent_ref, s32[96]{0:T(128)S(1)} %get-tuple-element.278.off_ref, f32[8,2,12,104,128]{4,3,2,1,0:T(8,128)S(1)} %bitcast.29, f32[8,2,12,104,128]{4,3,2,1,0:T(8,128)S(1)} %bitcast.30, f32[8,2,12,104,128]{4,3,2,1,0:T(8,128)S(1)} %bitcast.31, ...), custom_call_target="tpu_custom_call" | custom-call | flops 1258291200 | bytes 19660800 | tf_op jit(solution)/shard_map/contract_pairs/pallas_call | solution.py:184
  145.3 0.1 collective-permute-start.1
  145.4 0.0 copy-done.6
  145.4 0.1 eq.100
  145.5 0.0 copy-done.5
  145.5 0.2 convert_reduce_fusion
  145.7 0.6 reduce_max.9
  146.3 4.9 %pmax.7 = s32[]{:T(128)} all-reduce(s32[]{:T(128)} %reduce_max.9), channel_id=1, replica_groups=mesh['mol'=2,'amp'=4,'summa'=2,'rep'=2] {'mol'}, use_global_device_ids=true, to_apply=%region_4.5 | all-reduce | flops 1 | bytes 8 | tf_op jit(solution)/shard_map/pmax | solution.py:236
  151.2 14.5 %collective-permute-done.1.refs_9_ = f32[100,8,256]{2,1,0:T(8,128)S(1)} collective-permute-done((f32[100,8,256]{2,1,0:T(8,128)S(1)}, f32[100,8,256]{2,1,0:T(8,128)S(1)}, u32[]{:S(2)}, u32[]{:S(2)}) %collective-permute-start.1) | collective-permute-done | bytes 819232 | tf_op jit(solution)/shard_map/ppermute | solution.py:231
  165.8 0.0 copy-start.3
  165.8 3.9 %copy-done.3 = f32[16,12,104,128]{3,2,1,0:T(8,128)S(1)} copy-done((f32[16,12,104,128]{3,2,1,0:T(8,128)S(1)}, f32[16,12,104,128]{3,2,1,0:T(8,128)}, u32[]{:S(2)}) %copy-start.3) | copy-done | bytes 10223640
  169.7 30.5 %contract_pairs.13 = f32[2,100,8,100]{3,2,1,0:T(8,128)S(1)} custom-call(s32[96]{0:T(128)S(1)} %get-tuple-element.279.ent_ref, s32[96]{0:T(128)S(1)} %get-tuple-element.278.off_ref, f32[8,2,12,104,128]{4,3,2,1,0:T(8,128)S(1)} %bitcast.37, f32[8,2,12,104,128]{4,3,2,1,0:T(8,128)S(1)} %bitcast.38, f32[8,2,12,104,128]{4,3,2,1,0:T(8,128)S(1)} %bitcast.39, ...), custom_call_target="tpu_custom_call" | custom-call | flops 1258291200 | bytes 19660800 | tf_op jit(solution)/shard_map/contract_pairs/pallas_call | solution.py:184
  200.2 0.6 while.14
  200.8 0.0 copy-start.4
  200.8 0.9 copy-done.4
  (5 shorter events, 0.0 us)
Async XLA Ops:
  6.5 105.0 %all-gather.8.cloned.1.call-start = ((), (), s32[]{:S(2)}) async-start(), calls=%async_computation | async-start | bytes 11501568 | tf_op jit(solution)/shard_map/all_gather | solution.py:223
  111.6 3.9 %copy-start.2 = (f32[16,12,104,128]{3,2,1,0:T(8,128)S(1)}, f32[16,12,104,128]{3,2,1,0:T(8,128)}, u32[]{:S(2)}) copy-start(f32[16,12,104,128]{3,2,1,0:T(8,128)} %all-gather.8.cloned.1.call-done) | copy-start | bytes 30670852
  115.5 29.9 %copy-start.6 = (s32[100]{0:T(128)S(1)}, s32[100]{0:T(128)}, u32[]{:S(2)}) copy-start(s32[100]{0:T(128)} %param.8) | copy-start | bytes 1204
  115.5 30.0 %copy-start.5 = (s32[8]{0:T(128)S(1)}, s32[8]{0:T(128)}, u32[]{:S(2)}) copy-start(s32[8]{0:T(128)} %param.9) | copy-start | bytes 100
  145.3 20.5 %collective-permute-start.1 = (f32[100,8,256]{2,1,0:T(8,128)S(1)}, f32[100,8,256]{2,1,0:T(8,128)S(1)}, u32[]{:S(2)}, u32[]{:S(2)}) collective-permute-start(f32[100,8,256]{2,1,0:T(8,128)S(1)} %contract_pairs.12), channel_id=1, source_target_pairs={{0,2},{2,0},{1,3},{3,1},{4,6},{6,4},{5,7},{7,5},{8,10},{10,8},{9,1... | collective-permute-start | bytes 2457608 | tf_op jit(solution)/shard_map/ppermute | solution.py:231
  165.8 3.9 %copy-start.3 = (f32[16,12,104,128]{3,2,1,0:T(8,128)S(1)}, f32[16,12,104,128]{3,2,1,0:T(8,128)}, u32[]{:S(2)}) copy-start(f32[16,12,104,128]{3,2,1,0:T(8,128)} %all-gather.8.cloned.1.call-done) | copy-start | bytes 30670852
  200.8 0.9 copy-start.4
Sparse Core Ops, SparseCore 0:
  13.3 98.1 all-gather.7

commit v2 on v0

v2 whole, which is shorter than its diff:
```python
import functools
import math

import jax
import jax.numpy as jnp
from jax import lax
from jax.experimental import pallas as pl
from jax.experimental.pallas import tpu as pltpu
from jax.sharding import PartitionSpec as P

CAP = 12
RING = 5
OWN = 16
DEPTH = 4
LANES = 128
VMEM_LIMIT = 60 * 1024 * 1024


def round_up(value, unit):
    return -(-value // unit) * unit


def pack_kernel(groups, tile, cuts, pos_ref, occ_ref, virt_ref, src_ref, *refs):
    outs, (buf, stage, sems, out_sems) = refs[:-4], refs[-4:]
    slots, c_blk, rows_a, inner = buf.shape
    k_local, c_local = src_ref.shape[:2]
    blocks = c_local // c_blk
    per_group = rows_a // groups
    me, mine, start = pos_ref[0], pos_ref[1], pos_ref[2]

    def look(ent, found):
        k, block = (ent, 0) if blocks == 1 else (ent // blocks, ent % blocks)
        same = occ_ref[me * k_local + k] == virt_ref[(mine * c_local + block * c_blk) // tile]
        slot = found - start

        @pl.when(same & (slot >= 0) & (slot < slots))
        def _():
            rows = pl.ds(pl.multiple_of(block * c_blk, c_blk), c_blk)
            pltpu.make_async_copy(src_ref.at[k, rows], buf.at[slot], sems.at[slot]).start()

        return found + same.astype(jnp.int32)

    found = lax.fori_loop(0, k_local * blocks, look, jnp.int32(0))

    @pl.loop(0, jnp.clip(found - start, 0, slots))
    def _(slot):
        pltpu.make_async_copy(src_ref.at[0, pl.ds(0, c_blk)], buf.at[slot], sems.at[slot]).wait()
        for a in range(rows_a):
            phase = lax.rem(a // per_group - me + groups, groups)
            lane = (a % per_group) * c_blk
            stage[phase, slot, :inner, lane : lane + c_blk] = buf[slot, :, a, :].T

    copies = []
    for i, (out, (first, last)) in enumerate(zip(outs, cuts)):
        view = stage.at[:, pl.ds(first, last - first)]
        copies.append(pltpu.make_async_copy(view, out, out_sems.at[i]))
        copies[-1].start()
    for one in copies:
        one.wait()


def pack(integrals, occ, virt, pos, groups, c_blk, tile, cuts):
    _, _, rows_a, inner = integrals.shape
    slots = cuts[-1][1]
    shape = (round_up(inner, 8), rows_a // groups * c_blk)
    smem = pl.BlockSpec(memory_space=pltpu.SMEM)
    hbm = pl.BlockSpec(memory_space=pltpu.HBM)
    return pl.pallas_call(
        functools.partial(pack_kernel, groups, tile, cuts),
        out_shape=[jax.ShapeDtypeStruct((groups, last - first) + shape, jnp.float32) for first, last in cuts],
        in_specs=[smem, smem, smem, hbm],
        out_specs=[hbm] * len(cuts),
        scratch_shapes=[
            pltpu.VMEM((slots, c_blk, rows_a, inner), jnp.float32),
            pltpu.VMEM((groups, slots) + shape, jnp.float32),
            pltpu.SemaphoreType.DMA((slots,)),
            pltpu.SemaphoreType.DMA((len(cuts),)),
        ],
        compiler_params=pltpu.CompilerParams(vmem_limit_bytes=VMEM_LIMIT),
        name="pack_pairs",
    )(pos, occ, virt, integrals)


def plan_kernel(chips, k_local, c_local, c_blk, tile, pos_ref, occ_ref, virt_ref, after_ref, out_ref, spares):
    del after_ref
    blocks = c_local // c_blk
    me, mine = pos_ref[0], pos_ref[1]
    z, core = mine // 2, lax.rem(mine, 2)

    @pl.loop(0, 2 * chips)
    def _(d):
        def look(ent, found):
            k, block = (ent, 0) if blocks == 1 else (ent // blocks, ent % blocks)
            same = occ_ref[me * k_local + k] == virt_ref[(d * c_local + block * c_blk) // tile]
            return found + same.astype(jnp.int32)

        spares[d] = jnp.maximum(lax.fori_loop(0, k_local * blocks, look, jnp.int32(0), unroll=5) - RING, 0)

    def share(chip):
        return (spares[2 * chip] + spares[2 * chip + 1] + 1 - core) // 2

    def add(chip, held):
        one = share(chip)
        return held[0] + jnp.where(chip >= z, one, 0), held[1] + jnp.where(chip <= z, one, 0)

    held = lax.fori_loop(0, chips, add, (jnp.int32(0), jnp.int32(0)))
    for h in range(1, chips):
        for way, sender in enumerate([chips - h, h - 1]):
            row = [core, spares[2 * z], share(z), jnp.where(z == sender, held[way], 0)]
            for i, value in enumerate(row):
                out_ref[((h - 1) * 2 + way) * 4 + i] = value


def plan(pos, occ, virt, after, chips, k_local, c_local, c_blk, tile):
    smem = pl.BlockSpec(memory_space=pltpu.SMEM)
    return pl.pallas_call(
        functools.partial(plan_kernel, chips, k_local, c_local, c_blk, tile),
        out_shape=jax.ShapeDtypeStruct(((chips - 1) * 8,), jnp.int32),
        in_specs=[smem, smem, smem, pl.BlockSpec(memory_space=pltpu.HBM)],
        out_specs=smem,
        scratch_shapes=[pltpu.SMEM((2 * chips,), jnp.int32)],
        name="plan_messages",
    )(pos, occ, virt, after)


def gate_kernel(n_got, n_held, n_out, split, hop, info_ref, own_ref, other_ref, *refs):
    got = refs[:n_got]
    outs = refs[n_got + n_held : n_got + n_held + n_out]
    stage, sems, out_sems = refs[-3:]
    cap = sems.shape[1]
    groups = own_ref.shape[0]
    if not n_out:
        return

    for step in range(2):
        for way in range(2):
            core, first_count, share, total = (info_ref[((hop - 1) * 2 + way) * 4 + i] for i in range(4))

            @pl.loop(0, jnp.minimum(total, cap))
            def _(slot):
                dst, sem = stage.at[way, :, slot], sems.at[way, slot]
                if step:
                    pltpu.make_async_copy(own_ref.at[:, 0], dst, sem).wait()
                    return
                place = 2 * slot + core
                second = (place >= first_count).astype(jnp.int32)
                rank = place - second * first_count

                @pl.when((slot < share) & (second == core))
                def _():
                    pltpu.make_async_copy(own_ref.at[:, rank], dst, sem).start()

                @pl.when((slot < share) & (second != core))
                def _():
                    pltpu.make_async_copy(other_ref.at[:, rank], dst, sem).start()

                if got:

                    @pl.when(slot >= share)
                    def _():
                        pltpu.make_async_copy(got[way].at[:, slot - share], dst, sem).start()

    def put(way, i):
        view = stage.at[way, i % groups] if split else stage.at[way]
        return pltpu.make_async_copy(view, outs[i], out_sems.at[i])

    for action in range(2):
        for i in range(n_out):
            way = i // groups if split else i

            @pl.when(info_ref[((hop - 1) * 2 + way) * 4 + 3] > 0)
            def _():
                put(way, i).wait() if action else put(way, i).start()


def gate(info, own, other, got, cap, split, held, hop=1):
    groups, _, *tile = own.shape
    hbm = pl.BlockSpec(memory_space=pltpu.HBM)
    out = [(cap, *tile)] * (2 * groups) if split else [(groups, cap, *tile)] * 2
    if not cap:
        out = []
    n_in = 3 + len(got)
    done = pl.pallas_call(
        functools.partial(gate_kernel, len(got), len(held), len(out), split, hop),
        out_shape=[jax.ShapeDtypeStruct(shape, jnp.float32) for shape in out]
        + [jax.ShapeDtypeStruct(one.shape, one.dtype) for one in held],
        in_specs=[pl.BlockSpec(memory_space=pltpu.SMEM)] + [hbm] * (n_in - 1 + len(held)),
        out_specs=[hbm] * (len(out) + len(held)),
        scratch_shapes=[
            pltpu.VMEM((2, groups, max(cap, 1), *tile), jnp.float32),
            pltpu.SemaphoreType.DMA((2, max(cap, 1))),
            pltpu.SemaphoreType.DMA((max(len(out), 1),)),
        ],
        input_output_aliases={n_in + i: len(out) + i for i in range(len(held))},
        compiler_params=pltpu.CompilerParams(vmem_limit_bytes=VMEM_LIMIT),
        name="next_step",
    )(info, own, other, *got, *held)
    return done[: len(out)], done[len(out) :]


def contract_kernel(views, final, c_blk, n_acc, width, ent_ref, off_ref, *refs):
    n_src = len(views)
    srcs, amp_ref, adds = refs[:n_src], refs[n_src], refs[n_src + 1 : n_src + 1 + n_acc]
    out_refs = refs[n_src + 1 + n_acc : n_src + 1 + n_acc + width]
    wall, tbuf, rhs, todo, held_at, found, wsem, tsem, *rest = refs[n_src + 1 + n_acc + width :]
    accs = rest if final else out_refs
    inner = wall.shape[2]
    _, shares, cols_j, cols_b, window = tbuf.shape
    per_group = accs[0].shape[2] // LANES

    for part in range(shares + 1):
        found[part] = 0
    for ref, (lead, start, count, base) in zip(srcs, views):

        @pl.loop(0, count)
        def _(slot, ref=ref, lead=lead, start=start, base=base):
            @pl.when(ent_ref[start + slot] >= 0)
            def _():
                part = lax.rem(off_ref[start + slot] // c_blk, shares)
                at, held = found[part], found[shares]
                todo[part, at] = start + slot
                held_at[part, at] = held
                found[part] = at + 1
                found[shares] = held + 1
                dst = wall.at[held] if width > 1 else wall.at[held, 0]
                pltpu.make_async_copy(ref.at[lead + (base + slot,)], dst, wsem.at[held]).start()

    counts = [found[part] for part in range(shares)]
    total = functools.reduce(jnp.maximum, counts)

    def fetch(i, part):
        slot = todo[part, i]
        place = lax.rem(i, DEPTH)
        first = pl.multiple_of((off_ref[slot] // window) * window, window)
        return pltpu.make_async_copy(
            amp_ref.at[ent_ref[slot], :, :, pl.ds(first, window)], tbuf.at[place, part], tsem.at[place, part]
        )

    def start(i):
        for part in range(shares):

            @pl.when(i < counts[part])
            def _():
                fetch(i, part).start()

    for i in range(DEPTH - 1):
        start(jnp.int32(i))
    rhs[...] = jnp.zeros_like(rhs)
    for n, acc in enumerate(accs):
        mine = adds[n::width]
        value = mine[0][...] if mine else jnp.zeros(acc.shape, jnp.float32)
        for one in mine[1:]:
            value += one[...]
        acc[...] = value

    @pl.loop(0, total)
    def _(i):
        start(i + DEPTH - 1)
        place = lax.rem(i, DEPTH)
        for part in range(shares):
            live = i < counts[part]
            held = jnp.where(live, held_at[part, i], 0)

            @pl.when(live)
            def _():
                dst = wall.at[held] if width > 1 else wall.at[held, 0]
                pltpu.make_async_copy(srcs[0].at[views[0][0] + (0,)], dst, wsem.at[held]).wait()

            for n in range(width):
                w = wall[held, n].T
                w = jnp.where(jnp.full(w.shape, i, jnp.int32) < counts[part], w, 0.0)
                for a in range(per_group):
                    one = w[a * c_blk : (a + 1) * c_blk]
                    high = one.astype(jnp.bfloat16)
                    low = (one - high.astype(jnp.float32)).astype(jnp.bfloat16)
                    lane = (n * per_group + a) * LANES
                    lane = slice(lane, lane + inner)
                    for copy, value in enumerate([high, high, low]):
                        row = copy * window + part * c_blk
                        rhs[row : row + c_blk, lane] = value
        x = jnp.zeros((cols_j * cols_b, window), jnp.float32)
        lane = lax.broadcasted_iota(jnp.int32, x.shape, 1)
        for part in range(shares):

            @pl.when(i < counts[part])
            def _():
                fetch(i, part).wait()

            limit = jnp.where(i < counts[part], (part + 1) * c_blk, 0)
            mask = (lane >= part * c_blk) & (lane < limit)
            x = jnp.where(mask, tbuf[place, part].reshape(x.shape), x)
        high = x.astype(jnp.bfloat16)
        low = (x - high.astype(jnp.float32)).astype(jnp.bfloat16)
        lhs = jnp.concatenate([high, low, high], axis=1)
        prod = jnp.dot(lhs, rhs[...], preferred_element_type=jnp.float32)
        for n, acc in enumerate(accs):
            lanes = per_group * LANES
            acc[...] += prod[:, n * lanes : (n + 1) * lanes].reshape(acc.shape)

    if final:
        (out_ref,), (acc,) = out_refs, accs
        rows = out_ref.shape[1]
        for a in range(per_group):
            for b in range(cols_b):
                out_ref[a, :, b, :] = acc[:, b, a * LANES : (a + 1) * LANES].T[:rows]


def contract(sources, views, ent, off, amplitudes, c_blk, adds=(), final=None, width=1):
    _, cols_j, cols_b, _ = amplitudes.shape
    rows, lanes = sources[0].shape[-2:]
    per_group = lanes // c_blk
    slots = sum(view[2] for view in views)
    window = max(LANES, c_blk)
    shares = window // c_blk
    held = [jax.ShapeDtypeStruct((cols_j, cols_b, per_group * LANES), jnp.float32)] * width
    smem = pl.BlockSpec(memory_space=pltpu.SMEM)
    hbm = pl.BlockSpec(memory_space=pltpu.HBM)
    vmem = pl.BlockSpec(memory_space=pltpu.VMEM)
    scratch = [
        pltpu.VMEM((slots, width, rows, lanes), jnp.float32),
        pltpu.VMEM((DEPTH, shares, cols_j, cols_b, window), jnp.float32),
        pltpu.VMEM((3 * window, width * per_group * LANES), jnp.bfloat16),
        pltpu.SMEM((shares, slots), jnp.int32),
        pltpu.SMEM((shares, slots), jnp.int32),
        pltpu.SMEM((shares + 1,), jnp.int32),
        pltpu.SemaphoreType.DMA((slots,)),
        pltpu.SemaphoreType.DMA((DEPTH, shares)),
    ]
    if final is not None:
        scratch.append(pltpu.VMEM(held[0].shape, jnp.float32))
        held = [jax.ShapeDtypeStruct((per_group, final, cols_b, cols_j), jnp.float32)]
    return pl.pallas_call(
        functools.partial(contract_kernel, views, final is not None, c_blk, len(adds), width),
        out_shape=held,
        in_specs=[smem, smem] + [hbm] * (len(sources) + 1) + [vmem] * len(adds),
        out_specs=[vmem] * width,
        scratch_shapes=scratch,
        compiler_params=pltpu.CompilerParams(vmem_limit_bytes=VMEM_LIMIT),
        cost_estimate=pl.CostEstimate(
            flops=width * slots * cols_j * cols_b * per_group * LANES * c_blk,
            bytes_accessed=slots * cols_j * cols_b * LANES * 2,
            transcendentals=0,
        ),
        name="contract_pairs",
    )(ent, off, *sources, amplitudes, *adds)


def spare_caps(hops, scale):
    return [math.ceil(scale * (2.0 * h + 4.3 * math.sqrt(h))) for h in range(1, hops + 1)]


def body(integrals, amplitudes, occ_irreps, virt_irreps):
    k_local, c_local, rows_a, inner = integrals.shape
    groups = lax.axis_size("summa")
    chips = lax.axis_size("amp")
    cores = lax.axis_size("rep")
    parts = chips * cores
    me = lax.axis_index("summa")
    z = lax.axis_index("amp")
    core = lax.axis_index("rep")
    mine = z * cores + core
    tile = parts * c_local // virt_irreps.shape[0]
    c_blk = min(tile, c_local)
    blocks = c_local // c_blk
    entries = k_local * blocks

    turned = jnp.transpose(amplitudes, (0, 3, 1, 2))
    entry = jnp.arange(entries, dtype=jnp.int32)
    device = jnp.arange(parts, dtype=jnp.int32)

    def swap(value):
        return lax.ppermute(value, "rep", [(0, 1), (1, 0)])

    ways = [-1, 1]

    def along(way, value, sources):
        return lax.ppermute(value, "amp", [(i, i + ways[way]) for i in sources])

    def packed(start, cuts):
        pos = jnp.stack([me, mine, jnp.asarray(start, jnp.int32)])
        return pos, pack(integrals, occ_irreps, virt_irreps, pos, groups, c_blk, tile, cuts)

    hops = chips - 1
    spare = OWN - RING
    caps = spare_caps(hops, entries / 50)
    pos, (ring, spares) = packed(0, [(0, RING), (RING, OWN)])
    info = plan(pos, occ_irreps, virt_irreps, ring, chips, k_local, c_local, c_blk, tile)
    sister_spares, sister_ring = swap(spares), swap(ring)
    last = [along(way, ring, [range(1, chips), range(chips - 1)][way]) for way in range(2)]
    held = [*last, ring, sister_ring]
    sent, held = gate(info, spares, sister_spares, [], caps[0], False, held)
    last, (ring, sister_ring) = held[:2], held[2:]

    occ = lax.dynamic_slice_in_dim(occ_irreps, me * k_local, k_local)
    block_labels = jnp.repeat(virt_irreps, tile // c_blk).reshape(parts, blocks)
    allowed = (occ[:, None, None] == block_labels.T[None]).reshape(entries, parts)
    ranks = jnp.cumsum(allowed.astype(jnp.int32), axis=0) - 1
    counts = ranks[-1] + 1

    def places(ident):
        ent, dev = ident // parts, ident % parts
        k_of = jnp.where(ident < 0, -1, ent // blocks)
        return k_of, jnp.where(ident < 0, 0, dev * c_local + (ent % blocks) * c_blk)

    def listed(where, count):
        hit = allowed[:, :, None] & (where[:, :, None] == jnp.arange(count, dtype=jnp.int32))
        ident = entry[:, None] * parts + device
        return jnp.sum(jnp.where(hit, ident[:, :, None] + 1, 0), axis=(0, 1)) - 1

    def across(value, shift):
        return lax.ppermute(value, "summa", [(i, (i + shift) % groups) for i in range(groups)])

    def gather_round(start):
        panel = lax.all_gather(packed(start, [(0, CAP)])[1][0], ("amp", "rep"))
        inside = (ranks >= start) & (ranks < start + CAP)
        k_of, off = places(listed(jnp.where(inside, ranks - start + device * CAP, -1), parts * CAP))
        received = []
        for phase in [*range(1, groups), 0]:
            views = [((d, phase), d * CAP, CAP, 0) for d in range(parts)]
            if phase:
                received.append(across(contract([panel] * parts, views, k_of, off, turned, c_blk)[0], phase))
        return contract([panel] * parts, views, k_of, off, turned, c_blk, received, inner)[0]

    every = (occ_irreps[:, None, None] == block_labels.T[None]).reshape(groups, entries, parts)
    every = jnp.sum(every.astype(jnp.int32), axis=1)
    spare_all = jnp.maximum(every - RING, 0).reshape(groups, chips, cores)
    share_all = (spare_all.sum(2)[:, :, None] + 1 - jnp.arange(2, dtype=jnp.int32)) // 2
    ahead_all = jnp.cumsum(share_all[:, ::-1], axis=1)[:, ::-1]
    behind_all = jnp.cumsum(share_all, axis=1)
    fits = jnp.max(every) <= OWN
    for h in range(1, hops + 1):
        fits &= (jnp.max(ahead_all[:, chips - h]) <= caps[h - 1]) & (jnp.max(behind_all[:, h - 1]) <= caps[h - 1])
    own_verdict = jnp.stack([1 - fits.astype(jnp.int32), jnp.max(every)])
    verdict = own_verdict
    mols = lax.axis_size("mol")
    for shift in range(1, mols):
        turn = [(i, (i + shift) % mols) for i in range(mols)]
        verdict = jnp.maximum(verdict, lax.ppermute(own_verdict, "mol", turn))
    over, share, ahead, behind = spare_all[me], share_all[me], ahead_all[me], behind_all[me]

    base_ring, base_own = 0, 2 * hops * cores * RING
    base_sister = base_own + OWN
    base_chain = [[0] * (hops + 1) for _ in range(2)]
    total = base_sister + OWN
    for h in range(1, hops + 1):
        for way in range(2):
            base_chain[way][h] = total
            total += 2 * caps[h - 1]
    cap_at = jnp.array([0] + caps, jnp.int32)
    base_at = jnp.array(base_chain, jnp.int32)
    chip_of, core_of = device // cores, device % cores
    dz = chip_of - z
    way = (dz < 0).astype(jnp.int32)
    sister = (core_of != core).astype(jnp.int32)
    at_ring = base_ring + ((way * hops + jnp.abs(dz) - 1) * 2 + sister) * RING + ranks
    combined = ranks - RING + jnp.where(core_of == 1, over[:, 0][chip_of], 0)
    lane = combined % 2
    between_l = jnp.where((jnp.arange(chips) > z)[:, None], share, 0)
    between_l = jnp.cumsum(between_l, axis=0) - between_l
    between_r = jnp.where((jnp.arange(chips) < z)[:, None], share, 0)
    between_r = jnp.cumsum(between_r[::-1], axis=0)[::-1] - between_r
    between = jnp.where(dz[:, None] > 0, between_l[chip_of], between_r[chip_of])
    hop_at = jnp.where(way == 1, z, chips - 1 - z)
    at_chain = (
        base_at[way, hop_at]
        + jnp.where(lane != core, cap_at[hop_at], 0)
        + combined // 2
        + jnp.where(lane == 1, between[:, 1], between[:, 0])
    )
    at_chip = jnp.where(sister == 1, base_sister, base_own) + ranks
    where = jnp.where(dz == 0, at_chip, jnp.where(ranks < RING, at_ring, at_chain))
    k_of, off = places(listed(where, total))

    def sums(sources, **more):
        return contract([one[0] for one in sources], [one[1:] for one in sources], k_of, off, turned, c_blk, **more)

    every_group = (slice(None),)

    def joined(h):
        slots = [((way * hops + h - 1) * 2 * RING, RING) for way in range(2)]
        values = list(rings[h - 1])
        if h > 1:
            slots += [(base_chain[way][h - 1], caps[h - 2]) for way in range(2)]
            values += chain[h - 2]
        out, base = [], 0
        for value, (start, count) in zip(values, slots):
            out.append((value, every_group, start, count, 0))
            if len(swapped[h - 1]) > 1:
                out.append((swapped[h - 1][len(out) // 2], every_group, start + count, count, 0))
            else:
                out.append((swapped[h - 1][0], every_group, start + count, count, base))
            base += count
        return out

    rings, chain, swapped = [last], [], []
    ready = [
        (ring, every_group, base_own, RING, 0),
        (spares, every_group, base_own + RING, spare, 0),
        (sister_ring, every_group, base_sister, RING, 0),
        (sister_spares, every_group, base_sister + RING, spare, 0),
    ]
    early = []
    for h in range(2, hops + 1):
        sources = [range(1, chips - h + 1), range(h - 1, chips - 1)]
        last = [along(way, last[way], sources[way]) for way in range(2)]
        new = [along(0, sent[0], [chips - h + 1]), along(1, sent[1], [h - 2])]
        if chain:
            other = [swap(jnp.concatenate([*rings[-1], *chain[-1]], axis=1))]
        else:
            other = [swap(one) for one in rings[-1]]
        early = sums(ready, adds=early, width=groups)
        sent, held = gate(info, spares, sister_spares, new, caps[h - 1], h == hops, [*last, *other, *early, verdict], h)
        last, early, verdict = held[:2], held[-1 - groups : -1], held[-1]
        swapped.append(held[2 : -1 - groups])
        ready = joined(h - 1)
        chain.append(new)
        rings.append(last)
    swapped.append([swap(jnp.concatenate([*rings[-1], *chain[-1]], axis=1))])
    early = sums(ready + joined(hops), adds=early, width=groups)
    order = [*range(1, groups), 0]
    received = []
    waiting = sent
    for n, phase in enumerate(order):
        final = [along(way, waiting[way * groups + phase], [[1], [hops - 1]][way]) for way in range(2)]
        if n + 1 < groups:
            held = [*final, *waiting, *early]
            _, held = gate(info, spares, sister_spares, [], 0, False, held)
            final, waiting, early = held[:2], held[2:-groups], held[-groups:]
        other = [swap(one) for one in final]
        sources = []
        for way in range(2):
            start, cap = base_chain[way][hops], caps[-1]
            sources += [(final[way], (), start, cap, 0), (other[way], (), start + cap, cap, 0)]
        if phase:
            received.append(across(sums(sources, adds=[early[phase]])[0], phase))
        else:
            (first,) = sums(sources, adds=[early[phase], *received], final=inner)

    failed, most = verdict[0], verdict[1]

    def more(state):
        return state[0] < most

    def step(state):
        start, value = state
        return start + CAP, jnp.where(start == 0, 0.0, value) + gather_round(start)

    return lax.while_loop(more, step, (jnp.where(failed > 0, 0, most), first))[1]


def solution(mesh):
    return jax.shard_map(
        body,
        mesh=mesh,
        in_specs=(
            P(("mol", "summa"), ("amp", "rep"), None, None),
            P(("mol", "summa"), ("amp", "rep"), None, None),
            P("mol"),
            P("mol"),
        ),
        out_specs=P(("mol", "summa"), None, ("amp", "rep"), None),
        check_vma=False,
    )
```

time: 880 us -> 195 us (0.22)
  waiting for transfers between devices: 471 us -> 46.1 us
  matrix products: 355 us -> 0 us
  Pallas kernels: 0 us -> 81.8 us
  other arithmetic: 35.3 us -> 12.8 us
  starting transfers between devices: 0.04 us -> 22.5 us
  local copies, waits for them, and re-layouts: 2.94 us -> 14.4 us
    all_gather x1 -> x0, waiting for transfers between devices: 443 us -> none  [body(): panel = lax.all_gather(integrals, ('amp', 'rep'), axis=1, tiled=True)]
    dot_general x1 -> x0, matrix products: 355 us -> none  [contract(): jnp.einsum('kcai,kbcj->aibj', weights, amp_rows, precision=lax.Precision....]
    pallas_call x0 -> x11, Pallas kernels: none -> 81.8 us  [the longest x5 67.6 us: contract(): pl.pallas_call(functools.partial(contract_kernel, views, final is not Non...]
    ppermute x0 -> x26, waiting for transfers between devices: none -> 46.1 us  [the longest x14 31.9 us: along(): return lax.ppermute(value, 'amp', [(i, i + ways[way]) for i in sources])]
    mul x1, other arithmetic: 34.5 us -> 0.01 us  [listed(): ident = entry[:, None] * parts + device]
    reduce_scatter x1 -> x0, waiting for transfers between devices: 27.8 us -> none  [body(): lax.psum_scatter(partial_value, 'summa', scatter_dimension=0, tiled=True)]
    ppermute x0 -> x26, starting transfers between devices: none -> 22.5 us  [the longest x14 19.1 us: along(): return lax.ppermute(value, 'amp', [(i, i + ways[way]) for i in sources])]
    unnamed x0 -> x52, local copies, waits for them, and re-layouts: none -> 9.9 us
  transfers between devices with their start and end apart: 2 -> 26, of which waited for: 2 -> 7; matrix products, arithmetic and copies ran while one was open for 0% -> 6% of each run, Pallas kernels for 0% -> 29%
where the time goes in v2:
time: 195 us; the launch traced here: 198 us
  Pallas kernels  81.8 us (42%)
  waiting for transfers between devices  46.1 us (24%)
  starting transfers between devices  22.5 us (12%)
  between operations  19.6 us (10%)
  local copies, waits for them, and re-layouts  14.4 us (7%)
  other arithmetic  12.8 us (7%)
    pallas_call x5, Pallas kernels, contract(): pl.pallas_call(functools.partial(contract_kernel, views, final is not Non...  67.6 us
    ppermute x14, waiting for transfers between devices, along(): return lax.ppermute(value, 'amp', [(i, i + ways[way]) for i in sources])  31.9 us
    ppermute x14, starting transfers between devices, along(): return lax.ppermute(value, 'amp', [(i, i + ways[way]) for i in sources])  19.1 us
    unnamed x52, local copies, waits for them, and re-layouts  9.9 us
    ppermute x1, waiting for transfers between devices, across(): lax.ppermute(value, 'summa', [(i, (i + shift) % groups) for i in range(gr...  9.73 us
    pallas_call x1, Pallas kernels, pack(): pl.pallas_call(functools.partial(pack_kernel, groups, tile, cuts), out_sh...  5.93 us
    pallas_call x4, Pallas kernels, gate(): pl.pallas_call(functools.partial(gate_kernel, len(got), len(held), len(ou...  5.38 us
    ppermute x10, waiting for transfers between devices, swap(): return lax.ppermute(value, 'rep', [(0, 1), (1, 0)])  4.49 us
  transfers between devices with their start and end apart: 26, of which 7 were waited for; matrix products, arithmetic and copies ran while one was open for 6% of the time, Pallas kernels for 29%

profile of v2, /device:TPU:26, one launch (start us, length us, event | category | flops | bytes accessed | tf_op | source)
XLA Modules:
  0.0 198.1 jit_solution(1469752573408365125)
XLA Ops:
  7.1 5.9 %pack_pairs.6 = (f32[2,5,104,128]{3,2,1,0:T(8,128)}, f32[2,11,104,128]{3,2,1,0:T(8,128)}) custom-call(s32[3]{0:T(128)} %pad_add_fusion.1.pos_ref, s32[100]{0:T(128)} %occ_ref.3, s32[8]{0:T(128)} %virt_ref.3, f32[50,64,4,100]{3,2,1,0:T(4,128)} %src_ref.1), custom_call_target="tpu_custom_call" | custom-call | tf_op jit(solution)/shard_map/pack_pairs/pallas_call | solution.py:68
  13.1 1.3 collective-permute-start.2
  14.4 1.3 collective-permute-start.3
  16.8 0.7 fusion.30
  19.3 0.8 slice_reduce_fusion.3
  20.0 0.8 slice_reduce_fusion.2
  20.9 2.9 %plan_messages.1.info_ref = s32[24]{0:T(128)} custom-call(s32[3]{0:T(128)} %pad_add_fusion.1.pos_ref, s32[100]{0:T(128)S(1)} %copy-done.23, s32[8]{0:T(128)S(1)} %copy-done.22, f32[2,5,104,128]{3,2,1,0:T(8,128)} %get-tuple-element.259.after_ref.refs_2_), custom_call_target="tpu_custom_call" | custom-call | tf_op jit(solution)/shard_map/plan_messages/pallas_call | solution.py:116
  31.6 0.8 pad_add_fusion.2
  32.6 1.2 collective-permute-start.11
  33.8 0.8 copy-done.11
  34.9 1.1 copy-done.5
  36.0 2.8 %next_step.4 = (f32[2,7,104,128]{3,2,1,0:T(8,128)}, f32[2,7,104,128]{3,2,1,0:T(8,128)}, f32[2,5,104,128]{3,2,1,0:T(8,128)}, f32[2,5,104,128]{3,2,1,0:T(8,128)}, ...) custom-call(s32[24]{0:T(128)} %plan_messages.1.info_ref, ...), custom_call_target="tpu_custom_call", output_to_operand_aliasing={{2}: (3, {}), {3}: (4, {}), {4}: (5, {}), {5}: (6, {})} | custom-call | tf_op jit(solution)/shard_map/next_step/pallas_call | solution.py:183
  38.9 2.7 %collective-permute-start.5 = (f32[2,7,104,128]{3,2,1,0:T(8,128)}, f32[2,7,104,128]{3,2,1,0:T(8,128)S(1)}, u32[]{:S(2)}, u32[]{:S(2)}) collective-permute-start(f32[2,7,104,128]{3,2,1,0:T(8,128)} %get-tuple-element.261), channel_id=1, source_target_pairs={{12,8},{13,9},{14,10},{15,11},{28,24},{29,25},{30,26},{31,27}} | collective-permute-start | bytes 2236424 | tf_op jit(solution)/shard_map/ppermute | solution.py:377
  41.6 0.7 collective-permute-start.6
  42.4 1.3 collective-permute-start.8
  43.7 1.5 collective-permute-start.7
  46.3 1.3 fusion.32.refs_8_
  47.6 12.8 %contract_pairs.15 = (f32[100,8,256]{2,1,0:T(8,128)}, f32[100,8,256]{2,1,0:T(8,128)}) custom-call(s32[220]{0:T(256)} %get-tuple-element.462.ent_ref, s32[220]{0:T(256)} %get-tuple-element.461.off_ref, f32[2,5,104,128]{3,2,1,0:T(8,128)} %get-tuple-element.265.refs_0_, f32[2,11,104,128]{3,2,1,0:T(8,128)} %get-tuple-element.260.own_ref.refs_1_, ...), custom_call_target="tpu_custom_call" | custom-call | flops 838860800 | bytes 6553600 | tf_op jit(solution)/shard_map/contract_pairs/pallas_call | solution.py:332
  60.4 0.7 copy-done.15
  61.7 0.9 next_step.5
  62.6 3.3 %pad_maximum_fusion.1 = f32[2,24,104,128]{3,2,1,0:T(8,128)} fusion(f32[2,7,104,128]{3,2,1,0:T(8,128)} %copy-done.8, f32[2,7,104,128]{3,2,1,0:T(8,128)} %copy-done.7, f32[2,5,104,128]{3,2,1,0:T(8,128)} %get-tuple-element.272.refs_2_, f32[2,5,104,128]{3,2,1,0:T(8,128)} %get-tuple-element.271.refs_0_), kind=kLoop, calls=%fused_computation.28 | loop fusion | flops 1916928 | bytes 5111808 | tf_op jit(solution)/shard_map/concatenate | solution.py:508
  66.2 1.8 collective-permute-start.12
  68.0 1.7 collective-permute-start.13
  70.4 1.3 collective-permute-start.15
  71.7 8.8 %contract_pairs.16 = (f32[100,8,256]{2,1,0:T(8,128)}, f32[100,8,256]{2,1,0:T(8,128)}) custom-call(s32[220]{0:T(256)} %get-tuple-element.462.ent_ref, s32[220]{0:T(256)} %get-tuple-element.461.off_ref, f32[2,5,104,128]{3,2,1,0:T(8,128)} %get-tuple-element.263.refs_0_, f32[2,5,104,128]{3,2,1,0:T(8,128)} %get-tuple-element.273.refs_1_, ...), custom_call_target="tpu_custom_call" | custom-call | flops 524288000 | bytes 4096000 | tf_op jit(solution)/shard_map/contract_pairs/pallas_call | solution.py:332
  80.5 10.8 %collective-permute-done.15.refs_3_ = f32[2,5,104,128]{3,2,1,0:T(8,128)S(1)} collective-permute-done((f32[2,5,104,128]{3,2,1,0:T(8,128)}, f32[2,5,104,128]{3,2,1,0:T(8,128)S(1)}, u32[]{:S(2)}, u32[]{:S(2)}) %collective-permute-start.15) | collective-permute-done | bytes 532512 | tf_op jit(solution)/shard_map/ppermute | solution.py:377
  91.4 0.8 copy-done.10
  92.2 0.8 copy-done.2
  93.0 1.0 next_step.6
  94.0 2.2 %pad_maximum_fusion = f32[2,32,104,128]{3,2,1,0:T(8,128)S(1)} fusion(f32[2,11,104,128]{3,2,1,0:T(8,128)} %collective-permute-done.13.refs_1_.refs_14_, f32[2,11,104,128]{3,2,1,0:T(8,128)} %collective-permute-done.12.refs_0_.refs_12_, f32[2,5,104,128]{3,2,1,0:T(8,128)} %get-tuple-element.287.refs_10_, f32[2,5,104,128]{3,2,1,0:T(8,128)} %get-tuple-element.286.refs_8_), kind=kLoop, calls=%fused_computation.27 | loop fusion | flops 2555904 | bytes 6815744 | tf_op jit(solution)/shard_map/concatenate | solution.py:518
  96.3 1.6 collective-permute-start.17
  97.9 1.3 collective-permute-start.18
  99.1 3.1 %collective-permute-done.19.refs_9_.refs_11_.refs_13_.refs_15_ = f32[2,32,104,128]{3,2,1,0:T(8,128)S(1)} collective-permute-done((f32[2,32,104,128]{3,2,1,0:T(8,128)S(1)}, f32[2,32,104,128]{3,2,1,0:T(8,128)S(1)}, u32[]{:S(2)}, u32[]{:S(2)}) %collective-permute-start.19) | collective-permute-done | bytes 3407904 | tf_op jit(solution)/shard_map/ppermute | solution.py:372
  102.3 1.7 copy-done.3
  104.0 16.3 %contract_pairs.17 = (f32[100,8,256]{2,1,0:T(8,128)}, f32[100,8,256]{2,1,0:T(8,128)}) custom-call(s32[220]{0:T(256)} %get-tuple-element.462.ent_ref, s32[220]{0:T(256)} %get-tuple-element.461.off_ref, f32[2,5,104,128]{3,2,1,0:T(8,128)} %get-tuple-element.271.refs_0_, f32[2,24,104,128]{3,2,1,0:T(8,128)} %get-tuple-element.285.refs_1_.refs_3_.refs_5_.refs_7_, ...), custom_call_target="tpu_custom_call" | custom-call | flops 2936012800 | bytes 22937600 | tf_op jit(solution)/shard_map/contract_pairs/pallas_call | solution.py:332
  120.3 12.8 %collective-permute-done.18.refs_1_ = f32[14,104,128]{2,1,0:T(8,128)} collective-permute-done((f32[14,104,128]{2,1,0:T(8,128)}, f32[14,104,128]{2,1,0:T(8,128)}, u32[]{:S(2)}, u32[]{:S(2)}) %collective-permute-start.18) | collective-permute-done | bytes 745504 | tf_op jit(solution)/shard_map/ppermute | solution.py:377
  134.4 0.7 collective-permute-start.20
  135.1 1.3 collective-permute-start.22
  136.5 1.0 collective-permute-done.25.refs_3_
  137.4 0.9 copy-done.21
  138.3 14.8 %contract_pairs.18 = f32[100,8,256]{2,1,0:T(8,128)} custom-call(s32[220]{0:T(256)} %get-tuple-element.462.ent_ref, s32[220]{0:T(256)} %get-tuple-element.461.off_ref, f32[14,104,128]{2,1,0:T(8,128)} %get-tuple-element.295.refs_0_, f32[14,104,128]{2,1,0:T(8,128)} %copy-done.20, f32[14,104,128]{2,1,0:T(8,128)} %get-tuple-element.296.refs_2_, ...), custom_call_target="tpu_custom_call" | custom-call | flops 734003200 | bytes 11468800 | tf_op jit(solution)/shard_map/contract_pairs/pallas_call | solution.py:332
  153.5 8.2 %collective-permute-done.22.refs_2_ = f32[14,104,128]{2,1,0:T(8,128)S(1)} collective-permute-done((f32[14,104,128]{2,1,0:T(8,128)}, f32[14,104,128]{2,1,0:T(8,128)S(1)}, u32[]{:S(2)}, u32[]{:S(2)}) %collective-permute-start.22) | collective-permute-done | bytes 745504 | tf_op jit(solution)/shard_map/ppermute | solution.py:377
  161.7 0.7 fusion.31
  164.0 9.7 %collective-permute-done.26.refs_6_ = f32[100,8,256]{2,1,0:T(8,128)S(1)} collective-permute-done((f32[100,8,256]{2,1,0:T(8,128)}, f32[100,8,256]{2,1,0:T(8,128)S(1)}, u32[]{:S(2)}, u32[]{:S(2)}) %collective-permute-start.26) | collective-permute-done | bytes 819232 | tf_op jit(solution)/shard_map/ppermute | solution.py:411
  173.8 0.9 copy-done.16
  174.6 14.9 %contract_pairs.19 = f32[2,100,8,100]{3,2,1,0:T(8,128)S(1)} custom-call(s32[220]{0:T(256)} %get-tuple-element.462.ent_ref, s32[220]{0:T(256)} %get-tuple-element.461.off_ref, f32[14,104,128]{2,1,0:T(8,128)} %copy-done.17, f32[14,104,128]{2,1,0:T(8,128)} %copy-done.19, f32[14,104,128]{2,1,0:T(8,128)} %copy-done.18, ...), custom_call_target="tpu_custom_call" | custom-call | flops 734003200 | bytes 11468800 | tf_op jit(solution)/shard_map/contract_pairs/pallas_call | solution.py:332
  189.5 0.8 while.16
  190.4 0.9 copy-done.4
  (121 shorter events, 12.2 us)
Async XLA Ops:
  7.1 9.3 %copy-start.23 = (s32[100]{0:T(128)S(1)}, s32[100]{0:T(128)}, u32[]{:S(2)}) copy-start(s32[100]{0:T(128)} %occ_ref.3) | copy-start | bytes 1204
  7.1 9.4 %copy-start.22 = (s32[8]{0:T(128)S(1)}, s32[8]{0:T(128)}, u32[]{:S(2)}) copy-start(s32[8]{0:T(128)} %virt_ref.3) | copy-start | bytes 100
  7.1 23.1 %copy-start = (s32[4]{0:T(128)S(1)}, s32[4]{0:T(128)}, u32[]{:S(2)}) copy-start(s32[4]{0:T(128)} %constant.294.clone) | copy-start | bytes 52
  7.1 23.8 %copy-start.1 = (s32[2,4]{1,0:T(2,128)S(1)}, s32[2,4]{1,0:T(2,128)}, u32[]{:S(2)}) copy-start(s32[2,4]{1,0:T(2,128)} %constant.295.clone) | copy-start | bytes 100
  13.1 20.7 %collective-permute-start.2 = (f32[2,5,104,128]{3,2,1,0:T(8,128)}, f32[2,5,104,128]{3,2,1,0:T(8,128)S(1)}, u32[]{:S(2)}, u32[]{:S(2)}) collective-permute-start(f32[2,5,104,128]{3,2,1,0:T(8,128)} %get-tuple-element.259.after_ref.refs_2_), channel_id=1, source_target_pairs={{4,0},{8,4},{12,8},{5,1},{9,5},{13,9},{6,2},{10,6},{14,10},{7,3},{... | collective-permute-start | bytes 1597448 | tf_op jit(solution)/shard_map/ppermute | solution.py:377
  14.4 19.4 %collective-permute-start.3 = (f32[2,5,104,128]{3,2,1,0:T(8,128)}, f32[2,5,104,128]{3,2,1,0:T(8,128)S(1)}, u32[]{:S(2)}, u32[]{:S(2)}) collective-permute-start(f32[2,5,104,128]{3,2,1,0:T(8,128)} %get-tuple-element.259.after_ref.refs_2_), channel_id=1, source_target_pairs={{0,4},{4,8},{8,12},{1,5},{5,9},{9,13},{2,6},{6,10},{10,14},{3,7},{... | collective-permute-start | bytes 1597448 | tf_op jit(solution)/shard_map/ppermute | solution.py:377
  15.7 18.1 %collective-permute-start.4 = (f32[2,5,104,128]{3,2,1,0:T(8,128)}, f32[2,5,104,128]{3,2,1,0:T(8,128)S(1)}, u32[]{:S(2)}, u32[]{:S(2)}) collective-permute-start(f32[2,5,104,128]{3,2,1,0:T(8,128)} %get-tuple-element.259.after_ref.refs_2_), channel_id=1, source_target_pairs={{0,1},{1,0},{2,3},{3,2},{4,5},{5,4},{6,7},{7,6},{8,9},{9,8},{10,11... | collective-permute-start | bytes 1597448 | tf_op jit(solution)/shard_map/ppermute | solution.py:372
  16.4 17.4 %collective-permute-start.1 = (f32[2,11,104,128]{3,2,1,0:T(8,128)}, f32[2,11,104,128]{3,2,1,0:T(8,128)S(1)}, u32[]{:S(2)}, u32[]{:S(2)}) collective-permute-start(f32[2,11,104,128]{3,2,1,0:T(8,128)} %get-tuple-element.260.own_ref.refs_1_), channel_id=1, source_target_pairs={{0,1},{1,0},{2,3},{3,2},{4,5},{5,4},{6,7},{7,6},{8,9},{9,8},{10,11... | collective-permute-start | bytes 3514376 | tf_op jit(solution)/shard_map/ppermute | solution.py:372
  32.6 11.1 %collective-permute-start.11 = (s32[2]{0:T(128)S(1)}, s32[2]{0:T(128)S(1)}, u32[]{:S(2)}, u32[]{:S(2)}) collective-permute-start(s32[2]{0:T(128)S(1)} %pad_add_fusion.2), channel_id=1, source_target_pairs={{0,16},{16,0},{1,17},{17,1},{2,18},{18,2},{3,19},{19,3},{4,20},{20... | collective-permute-start | bytes 32 | tf_op jit(solution)/shard_map/ppermute | solution.py:438
  33.8 1.0 copy-start.12
  33.8 1.1 copy-start.13
  34.9 1.1 copy-start.5
  38.8 6.4 %collective-permute-start.10 = (f32[2,5,104,128]{3,2,1,0:T(8,128)}, f32[2,5,104,128]{3,2,1,0:T(8,128)S(1)}, u32[]{:S(2)}, u32[]{:S(2)}) collective-permute-start(f32[2,5,104,128]{3,2,1,0:T(8,128)} %get-tuple-element.264.refs_2_), channel_id=1, source_target_pairs={{0,1},{1,0},{2,3},{3,2},{4,5},{5,4},{6,7},{7,6},{8,9},{9,8},{10,11... | collective-permute-start | bytes 1597448 | tf_op jit(solution)/shard_map/ppermute | solution.py:372
  38.9 21.5 %collective-permute-start.5 = (f32[2,7,104,128]{3,2,1,0:T(8,128)}, f32[2,7,104,128]{3,2,1,0:T(8,128)S(1)}, u32[]{:S(2)}, u32[]{:S(2)}) collective-permute-start(f32[2,7,104,128]{3,2,1,0:T(8,128)} %get-tuple-element.261), channel_id=1, source_target_pairs={{12,8},{13,9},{14,10},{15,11},{28,24},{29,25},{30,26},{31,27}} | collective-permute-start | bytes 2236424 | tf_op jit(solution)/shard_map/ppermute | solution.py:377
  41.6 18.8 %collective-permute-start.6 = (f32[2,7,104,128]{3,2,1,0:T(8,128)}, f32[2,7,104,128]{3,2,1,0:T(8,128)S(1)}, u32[]{:S(2)}, u32[]{:S(2)}) collective-permute-start(f32[2,7,104,128]{3,2,1,0:T(8,128)} %get-tuple-element.262), channel_id=1, source_target_pairs={{0,4},{1,5},{2,6},{3,7},{16,20},{17,21},{18,22},{19,23}} | collective-permute-start | bytes 2236424 | tf_op jit(solution)/shard_map/ppermute | solution.py:377
  42.4 18.0 %collective-permute-start.8 = (f32[2,5,104,128]{3,2,1,0:T(8,128)}, f32[2,5,104,128]{3,2,1,0:T(8,128)}, u32[]{:S(2)}, u32[]{:S(2)}) collective-permute-start(f32[2,5,104,128]{3,2,1,0:T(8,128)} %get-tuple-element.264.refs_2_), channel_id=1, source_target_pairs={{4,8},{8,12},{5,9},{9,13},{6,10},{10,14},{7,11},{11,15},{20,24},{2... | collective-permute-start | bytes 1597448 | tf_op jit(solution)/shard_map/ppermute | solution.py:377
  43.7 16.6 %collective-permute-start.7 = (f32[2,5,104,128]{3,2,1,0:T(8,128)}, f32[2,5,104,128]{3,2,1,0:T(8,128)}, u32[]{:S(2)}, u32[]{:S(2)}) collective-permute-start(f32[2,5,104,128]{3,2,1,0:T(8,128)} %get-tuple-element.263.refs_0_), channel_id=1, source_target_pairs={{4,0},{8,4},{5,1},{9,5},{6,2},{10,6},{7,3},{11,7},{20,16},{24,20},... | collective-permute-start | bytes 1597448 | tf_op jit(solution)/shard_map/ppermute | solution.py:377
  45.2 15.2 %copy-start.14 = (f32[2,5,104,128]{3,2,1,0:T(8,128)}, f32[2,5,104,128]{3,2,1,0:T(8,128)S(1)}, u32[]{:S(2)}) copy-start(f32[2,5,104,128]{3,2,1,0:T(8,128)S(1)} %collective-permute-done.10.refs_5_) | copy-start | bytes 1597444
  45.2 15.2 %collective-permute-start.9 = (f32[2,5,104,128]{3,2,1,0:T(8,128)}, f32[2,5,104,128]{3,2,1,0:T(8,128)S(1)}, u32[]{:S(2)}, u32[]{:S(2)}) collective-permute-start(f32[2,5,104,128]{3,2,1,0:T(8,128)} %get-tuple-element.263.refs_0_), channel_id=1, source_target_pairs={{0,1},{1,0},{2,3},{3,2},{4,5},{5,4},{6,7},{7,6},{8,9},{9,8},{10,11... | collective-permute-start | bytes 1597448 | tf_op jit(solution)/shard_map/ppermute | solution.py:372
  60.4 1.0 copy-start.7
  60.4 1.2 copy-start.8
  65.9 25.4 %collective-permute-start.16 = (f32[2,24,104,128]{3,2,1,0:T(8,128)}, f32[2,24,104,128]{3,2,1,0:T(8,128)S(1)}, u32[]{:S(2)}, u32[]{:S(2)}) collective-permute-start(f32[2,24,104,128]{3,2,1,0:T(8,128)} %pad_maximum_fusion.1), channel_id=1, source_target_pairs={{0,1},{1,0},{2,3},{3,2},{4,5},{5,4},{6,7},{7,6},{8,9},{9,8},{10,11... | collective-permute-start | bytes 7667720 | tf_op jit(solution)/shard_map/ppermute | solution.py:372
  66.2 25.1 %collective-permute-start.12 = (f32[2,11,104,128]{3,2,1,0:T(8,128)}, f32[2,11,104,128]{3,2,1,0:T(8,128)}, u32[]{:S(2)}, u32[]{:S(2)}) collective-permute-start(f32[2,11,104,128]{3,2,1,0:T(8,128)} %get-tuple-element.269), channel_id=1, source_target_pairs={{8,4},{9,5},{10,6},{11,7},{24,20},{25,21},{26,22},{27,23}} | collective-permute-start | bytes 3514376 | tf_op jit(solution)/shard_map/ppermute | solution.py:377
  68.0 23.4 %collective-permute-start.13 = (f32[2,11,104,128]{3,2,1,0:T(8,128)}, f32[2,11,104,128]{3,2,1,0:T(8,128)}, u32[]{:S(2)}, u32[]{:S(2)}) collective-permute-start(f32[2,11,104,128]{3,2,1,0:T(8,128)} %get-tuple-element.270), channel_id=1, source_target_pairs={{4,8},{5,9},{6,10},{7,11},{20,24},{21,25},{22,26},{23,27}} | collective-permute-start | bytes 3514376 | tf_op jit(solution)/shard_map/ppermute | solution.py:377
  69.7 10.8 %collective-permute-start.14 = (f32[2,5,104,128]{3,2,1,0:T(8,128)}, f32[2,5,104,128]{3,2,1,0:T(8,128)S(1)}, u32[]{:S(2)}, u32[]{:S(2)}) collective-permute-start(f32[2,5,104,128]{3,2,1,0:T(8,128)} %get-tuple-element.271.refs_0_), channel_id=1, source_target_pairs={{4,0},{5,1},{6,2},{7,3},{20,16},{21,17},{22,18},{23,19}} | collective-permute-start | bytes 1597448 | tf_op jit(solution)/shard_map/ppermute | solution.py:377
  70.4 21.0 %collective-permute-start.15 = (f32[2,5,104,128]{3,2,1,0:T(8,128)}, f32[2,5,104,128]{3,2,1,0:T(8,128)S(1)}, u32[]{:S(2)}, u32[]{:S(2)}) collective-permute-start(f32[2,5,104,128]{3,2,1,0:T(8,128)} %get-tuple-element.272.refs_2_), channel_id=1, source_target_pairs={{8,12},{9,13},{10,14},{11,15},{24,28},{25,29},{26,30},{27,31}} | collective-permute-start | bytes 1597448 | tf_op jit(solution)/shard_map/ppermute | solution.py:377
  80.5 10.9 %copy-start.9 = (f32[2,5,104,128]{3,2,1,0:T(8,128)}, f32[2,5,104,128]{3,2,1,0:T(8,128)S(1)}, u32[]{:S(2)}) copy-start(f32[2,5,104,128]{3,2,1,0:T(8,128)S(1)} %collective-permute-done.14.refs_2_) | copy-start | bytes 1597444
  91.4 1.6 copy-start.2
  96.2 6.1 %collective-permute-start.19 = (f32[2,32,104,128]{3,2,1,0:T(8,128)S(1)}, f32[2,32,104,128]{3,2,1,0:T(8,128)S(1)}, u32[]{:S(2)}, u32[]{:S(2)}) collective-permute-start(f32[2,32,104,128]{3,2,1,0:T(8,128)S(1)} %pad_maximum_fusion), channel_id=1, source_target_pairs={{0,1},{1,0},{2,3},{3,2},{4,5},{5,4},{6,7},{7,6},{8,9},{9,8},{10,11... | collective-permute-start | bytes 10223624 | tf_op jit(solution)/shard_map/ppermute | solution.py:372
  96.3 24.1 %collective-permute-start.17 = (f32[14,104,128]{2,1,0:T(8,128)}, f32[14,104,128]{2,1,0:T(8,128)}, u32[]{:S(2)}, u32[]{:S(2)}) collective-permute-start(f32[14,104,128]{2,1,0:T(8,128)} %get-tuple-element.281.refs_3_), channel_id=1, source_target_pairs={{4,0},{5,1},{6,2},{7,3},{20,16},{21,17},{22,18},{23,19}} | collective-permute-start | bytes 2236424 | tf_op jit(solution)/shard_map/ppermute | solution.py:377
  97.9 35.3 %collective-permute-start.18 = (f32[14,104,128]{2,1,0:T(8,128)}, f32[14,104,128]{2,1,0:T(8,128)}, u32[]{:S(2)}, u32[]{:S(2)}) collective-permute-start(f32[14,104,128]{2,1,0:T(8,128)} %get-tuple-element.282.refs_5_), channel_id=1, source_target_pairs={{8,12},{9,13},{10,14},{11,15},{24,28},{25,29},{26,30},{27,31}} | collective-permute-start | bytes 2236424 | tf_op jit(solution)/shard_map/ppermute | solution.py:377
  102.3 1.7 copy-start.3
  133.9 2.6 %collective-permute-start.24 = (f32[14,104,128]{2,1,0:T(8,128)}, f32[14,104,128]{2,1,0:T(8,128)S(1)}, u32[]{:S(2)}, u32[]{:S(2)}) collective-permute-start(f32[14,104,128]{2,1,0:T(8,128)} %get-tuple-element.295.refs_0_), channel_id=1, source_target_pairs={{0,1},{1,0},{2,3},{3,2},{4,5},{5,4},{6,7},{7,6},{8,9},{9,8},{10,11... | collective-permute-start | bytes 2236424 | tf_op jit(solution)/shard_map/ppermute | solution.py:372
  133.9 3.5 %collective-permute-start.25 = (f32[14,104,128]{2,1,0:T(8,128)}, f32[14,104,128]{2,1,0:T(8,128)S(1)}, u32[]{:S(2)}, u32[]{:S(2)}) collective-permute-start(f32[14,104,128]{2,1,0:T(8,128)} %get-tuple-element.296.refs_2_), channel_id=1, source_target_pairs={{0,1},{1,0},{2,3},{3,2},{4,5},{5,4},{6,7},{7,6},{8,9},{9,8},{10,11... | collective-permute-start | bytes 2236424 | tf_op jit(solution)/shard_map/ppermute | solution.py:372
  134.4 18.8 %collective-permute-start.20 = (f32[14,104,128]{2,1,0:T(8,128)}, f32[14,104,128]{2,1,0:T(8,128)S(1)}, u32[]{:S(2)}, u32[]{:S(2)}) collective-permute-start(f32[14,104,128]{2,1,0:T(8,128)} %get-tuple-element.292), channel_id=1, source_target_pairs={{4,0},{5,1},{6,2},{7,3},{20,16},{21,17},{22,18},{23,19}} | collective-permute-start | bytes 2236424 | tf_op jit(solution)/shard_map/ppermute | solution.py:377
  135.1 26.5 %collective-permute-start.22 = (f32[14,104,128]{2,1,0:T(8,128)}, f32[14,104,128]{2,1,0:T(8,128)S(1)}, u32[]{:S(2)}, u32[]{:S(2)}) collective-permute-start(f32[14,104,128]{2,1,0:T(8,128)} %get-tuple-element.293), channel_id=1, source_target_pairs={{8,12},{9,13},{10,14},{11,15},{24,28},{25,29},{26,30},{27,31}} | collective-permute-start | bytes 2236424 | tf_op jit(solution)/shard_map/ppermute | solution.py:377
  136.4 1.0 copy-start.20
  137.4 0.9 copy-start.21
  138.3 23.3 %copy-start.26 = (s32[2]{0:T(128)S(1)}, s32[2]{0:T(128)}, u32[]{:S(2)}) copy-start(s32[2]{0:T(128)} %get-tuple-element.280) | copy-start | bytes 28
  153.2 20.6 %collective-permute-start.26 = (f32[100,8,256]{2,1,0:T(8,128)}, f32[100,8,256]{2,1,0:T(8,128)S(1)}, u32[]{:S(2)}, u32[]{:S(2)}) collective-permute-start(f32[100,8,256]{2,1,0:T(8,128)} %contract_pairs.18), channel_id=1, source_target_pairs={{0,2},{2,0},{1,3},{3,1},{4,6},{6,4},{5,7},{7,5},{8,10},{10,8},{9,1... | collective-permute-start | bytes 2457608 | tf_op jit(solution)/shard_map/ppermute | solution.py:411
  153.3 20.5 %copy-start.17 = (f32[14,104,128]{2,1,0:T(8,128)}, f32[14,104,128]{2,1,0:T(8,128)S(1)}, u32[]{:S(2)}) copy-start(f32[14,104,128]{2,1,0:T(8,128)S(1)} %collective-permute-done.20.refs_0_) | copy-start | bytes 2236420
  153.3 10.3 %collective-permute-start.21 = (f32[14,104,128]{2,1,0:T(8,128)S(1)}, f32[14,104,128]{2,1,0:T(8,128)S(1)}, u32[]{:S(2)}, u32[]{:S(2)}) collective-permute-start(f32[14,104,128]{2,1,0:T(8,128)S(1)} %collective-permute-done.20.refs_0_), channel_id=1, source_target_pairs={{0,1},{1,0},{2,3},{3,2},{4,5},{5,4},{6,7},{7,6},{8,9},{9,8},{10,11... | collective-permute-start | bytes 2236424 | tf_op jit(solution)/shard_map/ppermute | solution.py:372
  161.6 12.1 %copy-start.18 = (f32[14,104,128]{2,1,0:T(8,128)}, f32[14,104,128]{2,1,0:T(8,128)S(1)}, u32[]{:S(2)}) copy-start(f32[14,104,128]{2,1,0:T(8,128)S(1)} %collective-permute-done.22.refs_2_) | copy-start | bytes 2236420
  161.6 2.4 %collective-permute-start.23 = (f32[14,104,128]{2,1,0:T(8,128)S(1)}, f32[14,104,128]{2,1,0:T(8,128)}, u32[]{:S(2)}, u32[]{:S(2)}) collective-permute-start(f32[14,104,128]{2,1,0:T(8,128)S(1)} %collective-permute-done.22.refs_2_), channel_id=1, source_target_pairs={{0,1},{1,0},{2,3},{3,2},{4,5},{5,4},{6,7},{7,6},{8,9},{9,8},{10,11... | collective-permute-start | bytes 2236424 | tf_op jit(solution)/shard_map/ppermute | solution.py:372
  163.6 10.1 %copy-start.19 = (f32[14,104,128]{2,1,0:T(8,128)}, f32[14,104,128]{2,1,0:T(8,128)S(1)}, u32[]{:S(2)}) copy-start(f32[14,104,128]{2,1,0:T(8,128)S(1)} %collective-permute-done.21.refs_1_) | copy-start | bytes 2236420
  173.7 0.9 copy-start.16
  174.6 14.9 %copy-start.25 = (s32[50]{0:T(128)S(1)}, s32[50]{0:T(128)}, u32[]{:S(2)}) copy-start(s32[50]{0:T(128)} %copy-done.24) | copy-start | bytes 604
  190.3 0.9 copy-start.4
  (4 other events, 3.0 us)
